TPU v7x, 32 devices: a whole 2x2x4 slice. The times are simulated.
32 devices in a mesh: groups: 2 (over y), seq: 8 (over z, x), head: 1, sub: 2 (over core).
Axes of the slice: x: 2, y: 2, z: 4, core: 2. Of those that a mesh axis runs over, the one named last changes fastest.
Arguments:
- queries: bfloat16 [8, 32768, 512], P('head', ('groups', 'seq', 'sub')), parts along dimension 1, may hold values from -6 to 6
- keys: bfloat16 [8, 32768, 512], P('head', ('groups', 'seq', 'sub')), parts along dimension 1, may hold values from -6 to 6
- values: bfloat16 [8, 32768, 512], P('head', ('groups', 'seq', 'sub')), parts along dimension 1, may hold values from -6 to 6
- lr_codes: int32 [8, 32768], P('head', ('groups', 'seq', 'sub')), parts along dimension 1, may hold values from 0 to 15
- fast_gate: float32 [8, 512, 512], P('head', ('seq', 'sub')), may hold values from -0.25 to 0.25
- fast_up: float32 [8, 512, 512], P('head', ('seq', 'sub')), may hold values from -0.25 to 0.25
- fast_down: float32 [8, 512, 512], P('head', ('seq', 'sub')), may hold values from -0.25 to 0.25
Outputs:
- fast_out: bfloat16 [8, 32768, 512], P('head', ('groups', 'seq', 'sub')), parts along dimension 1
There are 2 independent parts, one for each index of `groups`. A program takes and returns all parts, laid end to end along the dimension named above; an argument that names none is the same for every part. Nothing has to cross between parts.
All inputs are finite; a program needn't handle non-finite values.
Results may differ from a plain program's by a relative error of at most 0.0085.
Values may be sent and summed in bfloat16 or wider, within the bound.
A program may use at most 192 MiB of HBM per device.

v0:
```python
import functools

import jax
import jax.numpy as jnp
from jax import lax
from jax.experimental import pallas as pl
from jax.experimental.pallas import tpu as pltpu
from jax.sharding import PartitionSpec as P

EPSILON = 1e-06
STEP_SIZE = 0.5
KIND = (0, 2, 1)
WIDTH = 2
VMEM_LIMIT = 60 * 1024 * 1024
BF = jnp.bfloat16
F32 = jnp.float32


def place():
    seq = lax.axis_index("seq")
    return lax.div(seq, WIDTH), lax.rem(seq, WIDTH), lax.axis_index("sub")


def device(z, x, s):
    return {"seq": z * WIDTH + x, "sub": s}


def greet(depth, z, x, s, others=()):
    barrier = pltpu.get_barrier_semaphore()
    partners = [device(lax.rem(z + k, depth), x, s) for k in range(1, depth)]
    partners += [device(z, 1 - x, s), device(z, x, 1 - s), *others]
    for partner in partners:
        pl.semaphore_signal(barrier, inc=1, device_id=partner, device_id_type=pl.DeviceIdType.MESH)
    pl.semaphore_wait(barrier, len(partners))


def send(src, dst, send_sem, recv_sem, target):
    return pltpu.make_async_remote_copy(
        src_ref=src,
        dst_ref=dst,
        send_sem=send_sem,
        recv_sem=recv_sem,
        device_id=target,
        device_id_type=pl.DeviceIdType.MESH,
    )


def dot(a, b, dims=((1,), (0,))):
    return lax.dot_general(a, b, (dims, ((), ())), preferred_element_type=F32)


def chain(depth, z, hop, started, unit, k):
    for back in (True, False):
        src = z - k if back else z + k
        onward = 1 if back else -1
        here = (src >= 0) if back else (src < depth)

        @pl.when(here)
        def _(src=src, onward=onward):
            hop(unit, src, -onward).wait_recv()
            started(unit, src)

            @pl.when((z + onward >= 0) & (z + onward < depth))
            def _():
                hop(unit, src, onward).start()


def chain_own(depth, z, hop, unit):
    for onward in (1, -1):

        @pl.when((z + onward >= 0) & (z + onward < depth))
        def _(onward=onward):
            hop(unit, z, onward).start()


def chain_sent(depth, z, hop, unit):
    for src in range(depth):

        @pl.when((src <= z) & (z < depth - 1))
        def _(src=src):
            hop(unit, src, 1).wait_send()

        @pl.when((src >= z) & (z > 0))
        def _(src=src):
            hop(unit, src, -1).wait_send()


def head_grads(k, values, codes, full, h, out):
    tokens, feats = k.shape
    half = feats // 2
    depth = full.shape[2]
    rates = (codes.astype(F32) + 1.0) / 16.0
    rates = jnp.transpose(jnp.broadcast_to(rates, (128, tokens)))
    rates = jnp.concatenate([rates] * (feats // 128), axis=1)
    target = (-rates * values.astype(F32)).astype(BF)
    for j in range(2):
        cols = pl.ds(j * half, half)
        gate = full[h, 0, :, :, :, :, cols].reshape(feats, half)
        up = full[h, 2, :, :, :, :, cols].reshape(feats, half)
        down = full[h, 1, pl.ds(j * (depth // 2), depth // 2)].reshape(half, feats)
        gate_pre = dot(k, gate)
        up_pre = dot(k, up)
        back = dot(target, down, ((1,), (1,)))
        sig = jax.nn.sigmoid(gate_pre)
        silu = gate_pre * sig
        hidden = (silu * up_pre).astype(BF)
        ggp = (back * up_pre * sig * (1.0 + gate_pre * (1.0 - sig))).astype(BF)
        gup = (back * silu).astype(BF)
        out[j, 0] = dot(k, ggp, ((0,), (0,))).astype(BF)
        out[j, 1] = dot(k, gup, ((0,), (0,))).astype(BF)
        gdown = dot(hidden, target, ((0,), (0,))).astype(BF)
        out[0, 2, cols, :] = gdown[:, :half]
        out[1, 2, cols, :] = gdown[:, half:]


def owner(depth, h):
    pos = h // WIDTH
    return jnp.where(pos % 2 == 0, pos // 2, depth - 1 - pos // 2)


def head_at(depth, h):
    return owner(depth, h) * WIDTH + h % WIDTH


def place_of(depth, z):
    return jnp.where(2 * z < depth, 2 * z, 2 * (depth - 1 - z) + 1)


def gather_kernel(
    depth, own, keys, values, codes, total, mine,
    full, kbuf, vbuf, obuf, got_c, paired, kept, got_x, summed, got_z,
    local, ksem, vsem, sr, sl, zr, xs, xr, ys, yr, cs, cr, gcs, gcr, gxs, gxr, gzs, gzr,
):
    heads = own.shape[0]
    z, x, s = place()
    y = lax.axis_index("groups")

    def load(h):
        slot = lax.rem(h, 2)
        return (
            pltpu.make_async_copy(keys.at[head_at(depth, h)], kbuf.at[slot], ksem.at[slot]),
            pltpu.make_async_copy(values.at[head_at(depth, h)], vbuf.at[slot], vsem.at[slot]),
        )

    for copy in load(0) + load(1):
        copy.start()
    pair = pl.ds(y, 2)
    keep = pltpu.make_async_copy(own.at[:, pair], full.at[:, pair, z, x, s], local)
    keep.start()
    greet(depth, z, x, s, ({"groups": 1 - y},))
    keep.wait()

    def hop(h, src, onward):
        block = full.at[h, pair, src, x, s]
        sems = sr if onward == 1 else sl
        return send(block, block, sems.at[h, src], zr.at[h, src], device(z + onward, x, s))

    def across(h, src):
        block = full.at[h, pair, src, x, s]
        return send(block, block, xs.at[h, src], xr.at[h, src], device(z, 1 - x, s))

    def over(h):
        block = full.at[h, 2 * y, :, :, s]
        return send(block, block, ys.at[h], yr.at[h], {"groups": 1 - y})

    def inside(h):
        block = full.at[h, :, :, :, s]
        return send(block, block, cs.at[h], cr.at[h], device(z, x, 1 - s))

    def first(h):
        chain_own(depth, z, hop, h)
        across(h, z).start()

    def hand(h):
        for src in range(depth):
            across(h, src).wait_recv()
        over(h).start()

    def spread(h):
        over(h).wait_recv()
        inside(h).start()

    def trade(h):
        return send(
            obuf.at[lax.rem(h, 2), 1 - s], got_c.at[h], gcs.at[h], gcr.at[h], device(z, x, 1 - s)
        )

    def deliver(zt, m):
        return send(
            paired.at[zt, m], got_x.at[zt, m], gxs.at[zt, m], gxr.at[zt, m], device(z, 1 - x, s)
        )

    def along(zt, m):
        return send(
            summed.at[zt, m], got_z.at[z, m], gzs.at[zt, m], gzr.at[z, m], device(zt, x, s)
        )

    def pair_up(h):
        zt = owner(depth, h)
        trade(h).wait_recv()
        slot = lax.rem(h, 2)
        ours = lax.rem(h, WIDTH) == x

        @pl.when(ours)
        def _():
            for m in range(3):
                kept[zt, m] = obuf[slot, s, m].astype(F32) + got_c[h, m].astype(F32)

        @pl.when(jnp.logical_not(ours))
        def _():
            for m in range(3):
                both = obuf[slot, s, m].astype(F32) + got_c[h, m].astype(F32)
                paired[zt, m] = both.astype(BF)
                deliver(zt, m).start()

    def join(h):
        zt = owner(depth, h)

        @pl.when(lax.rem(h, WIDTH) == WIDTH - 1)
        def _():
            @pl.when(zt == z)
            def _():
                for m in range(3):
                    deliver(zt, m).wait_recv()
                    total[m] = kept[zt, m] + got_x[zt, m].astype(F32)

            @pl.when(zt != z)
            def _():
                for m in range(3):
                    deliver(zt, m).wait_recv()
                    summed[zt, m] = (kept[zt, m] + got_x[zt, m].astype(F32)).astype(BF)
                    along(zt, m).start()

    def compute(h):
        slot = lax.rem(h, 2)
        inside(h).wait_recv()
        for copy in load(h):
            copy.wait()

        @pl.when(h >= 2)
        def _():
            trade(h - 2).wait_send()

        head_grads(kbuf[slot], vbuf[slot], codes[head_at(depth, h)], full, h, obuf.at[slot])
        trade(h).start()

        @pl.when(h + 2 < heads)
        def _():
            for copy in load(h + 2):
                copy.start()

    ahead = 2
    for h in range(ahead):
        first(h)

    def step(t, carry):
        def when(h, what):
            pl.when((h >= 0) & (h < heads))(lambda: what(h))

        when(t + ahead, first)
        when(t - depth, spread)
        when(t - depth + 1, hand)
        for k in range(depth - 1, 0, -1):
            when(t - k + 1, lambda h, k=k: chain(depth, z, hop, lambda u, i: across(u, i).start(), h, k))
        when(t - depth - 1, compute)
        when(t - depth - 2, pair_up)
        when(t - depth - 2 - late, join)
        return carry

    late = 2
    lax.fori_loop(0, heads + depth + 2 + late, step, 0)
    feats = mine.shape[1]
    for m in range(3):
        mine[m] = full[place_of(depth, z) * WIDTH + x, m].reshape(feats, feats)
    for k in range(1, depth):
        src = lax.rem(z + k, depth)
        for m in range(3):
            send(
                summed.at[src, m], got_z.at[src, m], gzs.at[src, m], gzr.at[src, m],
                device(src, x, s),
            ).wait_recv()
            total[m] += got_z[src, m].astype(F32)

    def last(h, carry):
        chain_sent(depth, z, hop, h)
        for src in range(depth):
            across(h, src).wait_send()
        over(h).wait_send()
        inside(h).wait_send()
        return carry

    lax.fori_loop(0, heads, last, 0)
    trade(heads - 2).wait_send()
    trade(heads - 1).wait_send()
    for zt in range(depth):
        for m in range(3):
            deliver(zt, m).wait_send()
            pl.when(zt != z)(lambda zt=zt, m=m: along(zt, m).wait_send())


def learn(own, keys, values, codes, depth):
    heads, kinds, rows, cols = own.shape
    tokens, feats = keys.shape[1:]
    dma = pltpu.SemaphoreType.DMA
    vmem = pl.BlockSpec(memory_space=pltpu.VMEM)
    anywhere = pl.BlockSpec(memory_space=pl.ANY)
    piece = (kinds, feats, feats // 2)
    return pl.pallas_call(
        functools.partial(gather_kernel, depth),
        out_shape=(
            jax.ShapeDtypeStruct(piece, F32),
            jax.ShapeDtypeStruct((kinds, feats, feats), BF),
        ),
        in_specs=[vmem, anywhere, anywhere, vmem],
        out_specs=(vmem, vmem),
        scratch_shapes=[
            pltpu.VMEM((heads, kinds, depth, WIDTH, 2, rows, cols), BF),
            pltpu.VMEM((2, tokens, feats), BF),
            pltpu.VMEM((2, tokens, feats), BF),
            pltpu.VMEM((2, 2) + piece, BF),
            pltpu.VMEM((heads,) + piece, BF),
            pltpu.VMEM((depth,) + piece, BF),
            pltpu.VMEM((depth,) + piece, F32),
            pltpu.VMEM((depth,) + piece, BF),
            pltpu.VMEM((depth,) + piece, BF),
            pltpu.VMEM((depth,) + piece, BF),
            dma(()),
            dma((2,)),
            dma((2,)),
            *[dma((heads, depth))] * 5,
            *[dma((heads,))] * 6,
            *[dma((depth, kinds))] * 4,
        ],
        compiler_params=pltpu.CompilerParams(
            collective_id=0, has_side_effects=True, vmem_limit_bytes=VMEM_LIMIT
        ),
        name="learn",
    )(own, keys, values, codes[:, None, :])


def apply_kernel(queries, weights, out):
    q = queries[0]
    half = weights.shape[-1]
    total = [None, None]
    for j in range(2):
        gate = dot(q, weights[0, j, 0])
        up = dot(q, weights[0, j, 1])
        hidden = (gate * jax.nn.sigmoid(gate) * up).astype(BF)
        for c in range(2):
            term = dot(hidden, weights[0, c, 2, pl.ds(j * half, half), :])
            total[c] = term if j == 0 else total[c] + term
    for c in range(2):
        out[0, :, pl.ds(c * half, half)] = total[c].astype(BF)


def apply_fast(queries, weights):
    heads, tokens, feats = queries.shape
    block = pl.BlockSpec((1, tokens, feats), lambda h: (h, 0, 0))
    return pl.pallas_call(
        apply_kernel,
        grid=(heads,),
        out_shape=jax.ShapeDtypeStruct(queries.shape, BF),
        in_specs=[
            block,
            pl.BlockSpec((1, 2, 3, feats, feats // 2), lambda h: (h, 0, 0, 0, 0)),
        ],
        out_specs=block,
        compiler_params=pltpu.CompilerParams(vmem_limit_bytes=VMEM_LIMIT),
        name="apply",
    )(queries, weights)


def renew_kernel(
    depth, total, weights, new, norm_out, norm_in, ns, nr, asr, asl, azr, axs, axr, acs, acr
):
    kinds, rows, half = total.shape
    z, x, s = place()
    greet(depth, z, x, s)
    for m in range(kinds):
        part = total[m]
        norm_out[m] = jnp.broadcast_to(jnp.sum(part * part, keepdims=True), norm_out.shape[1:])
    norms = send(norm_out, norm_in, ns, nr, device(z, x, 1 - s))
    norms.start()
    norms.wait()

    part = rows // 2
    units = ((2, part, rows - part, True), (2, 0, part, False), (0, 0, rows, False), (1, 0, rows, False))

    def block(u, src, col):
        m, begin, count, _ = units[u]
        return new.at[src, col, s, m, pl.ds(begin, count)]

    def hop(unit, src, onward):
        u, c = unit
        piece = block(u, src, 1 - x if c else x)
        sems = asr if onward == 1 else asl
        return send(piece, piece, sems.at[u, c, src], azr.at[u, c, src], device(z + onward, x, s))

    def share_x(u, src):
        piece = block(u, src, x)
        return send(piece, piece, axs.at[u, src], axr.at[u, src], device(z, 1 - x, s))

    def share_c(u, src):
        piece = block(u, src, slice(None))
        return send(piece, piece, acs.at[u, src], acr.at[u, src], device(z, x, 1 - s))

    def pass_on(u, src):
        if not units[u][3]:
            share_x(u, src).wait_recv()
        share_c(u, src).start()

    def arrived(unit, src):
        if not units[unit[0]][3]:
            share_x(unit[0], src).start()

    for m in (2, 0, 1):
        whole = weights[KIND[m]].astype(F32)
        weight_total = jnp.sum(whole * whole, keepdims=True)
        grad_total = norm_out[m, :1, :1] + norm_in[m, :1, :1]
        scale = STEP_SIZE * jnp.sqrt(weight_total + EPSILON) / jnp.sqrt(grad_total + EPSILON)
        own = weights[KIND[m], :, pl.ds(pl.multiple_of(s * half, half), half)].astype(F32)
        moved = own - scale * total[m]
        col_weight = jnp.sum(own * own, axis=0, keepdims=True)
        col_moved = jnp.sum(moved * moved, axis=0, keepdims=True)
        ratio = jnp.sqrt((col_weight + EPSILON) / (col_moved + EPSILON))
        new[z, x, s, m] = (moved * ratio).astype(BF)
        for u in range(len(units)):
            if units[u][0] == m:
                share_x(u, z).start()
                chain_own(depth, z, hop, (u, 0))
    share_x(0, z).wait_recv()
    chain_own(depth, z, hop, (0, 1))
    for k in range(1, depth + 1):
        for u in (1, 2, 3, 0):
            if k < depth:
                for c in range(2 if units[u][3] else 1):
                    chain(depth, z, hop, arrived, (u, c), k)
            if k == 1:
                pass_on(u, z)
            else:
                pl.when(z - k + 1 >= 0)(lambda u=u, k=k: pass_on(u, z - k + 1))
                pl.when(z + k - 1 < depth)(lambda u=u, k=k: pass_on(u, z + k - 1))

    for u in range(len(units)):
        for c in range(2 if units[u][3] else 1):
            chain_sent(depth, z, hop, (u, c))
        if units[u][3]:
            share_x(u, z).wait_send()
        for src in range(depth):
            if not units[u][3]:
                share_x(u, src).wait_send()
            share_c(u, src).wait()


def renew(total, weights, depth):
    kinds, rows, half = total.shape
    dma = pltpu.SemaphoreType.DMA
    piece = (kinds, rows, half)
    new = pl.pallas_call(
        functools.partial(renew_kernel, depth),
        out_shape=jax.ShapeDtypeStruct((depth, WIDTH, 2) + piece, BF),
        in_specs=[pl.BlockSpec(memory_space=pltpu.VMEM)] * 2,
        out_specs=pl.BlockSpec(memory_space=pltpu.VMEM),
        scratch_shapes=[
            pltpu.VMEM((kinds, 8, 128), F32),
            pltpu.VMEM((kinds, 8, 128), F32),
            dma(()),
            dma(()),
            *[dma((4, 2, depth))] * 3,
            *[dma((4, depth))] * 4,
        ],
        compiler_params=pltpu.CompilerParams(
            collective_id=1, has_side_effects=True, vmem_limit_bytes=VMEM_LIMIT
        ),
        name="renew",
    )(total, weights)
    return new.reshape((depth * WIDTH, 2) + piece)


def on_device_heads(depth, queries, keys, values, lr_codes, fast_gate, fast_up, fast_down):
    own = jnp.stack([fast_gate, fast_down, fast_up], axis=1).astype(BF)
    rows = [p // 2 if p % 2 == 0 else depth - 1 - p // 2 for p in range(depth)]
    order = [r * WIDTH + x for r in rows for x in range(WIDTH)]
    own = jnp.stack([own[h] for h in order])
    total, mine = learn(own, keys, values, lr_codes, depth)
    new = renew(total, mine, depth)
    return apply_fast(queries, new)


def column_squares(matrix):
    return jnp.sum(matrix * matrix, axis=1)


def rescale(moved, col_weight, col_moved):
    return moved * jnp.sqrt((col_weight + EPSILON) / (col_moved + EPSILON))[:, None, :]


def step_scale(col_weight, grad_total):
    return (
        STEP_SIZE * jnp.sqrt(jnp.sum(col_weight, axis=1) + EPSILON) / jnp.sqrt(grad_total + EPSILON)
    )


def apply_rows(queries, gate_b, up_b, down_b):
    query_gate = jnp.einsum("htd,hdf->htf", queries, gate_b, preferred_element_type=jnp.float32)
    query_up = jnp.einsum("htd,hdf->htf", queries, up_b, preferred_element_type=jnp.float32)
    query_hidden = (jax.nn.silu(query_gate) * query_up).astype(jnp.bfloat16)
    return jnp.einsum(
        "htf,hfd->htd", query_hidden, down_b, preferred_element_type=jnp.float32
    ).astype(jnp.bfloat16)


def local_grads_rows(keys, target, gate_b, up_b, down_b):
    gate_pre = jnp.einsum("htd,hdf->htf", keys, gate_b, preferred_element_type=jnp.float32)
    up_pre = jnp.einsum("htd,hdf->htf", keys, up_b, preferred_element_type=jnp.float32)
    sigmoid_gate = jax.nn.sigmoid(gate_pre)
    hidden = (gate_pre * sigmoid_gate * up_pre).astype(jnp.bfloat16)
    back = jnp.einsum("htd,hfd->htf", target, down_b, preferred_element_type=jnp.float32)
    grad_gate_pre = (back * up_pre * sigmoid_gate * (1.0 + gate_pre * (1.0 - sigmoid_gate))).astype(
        jnp.bfloat16
    )
    grad_up_pre = (back * gate_pre * sigmoid_gate).astype(jnp.bfloat16)
    grad_gate = jnp.einsum("htd,htf->hdf", keys, grad_gate_pre, preferred_element_type=jnp.float32)
    grad_up = jnp.einsum("htd,htf->hdf", keys, grad_up_pre, preferred_element_type=jnp.float32)
    grad_down = jnp.einsum("htf,htd->hfd", hidden, target, preferred_element_type=jnp.float32)
    return (grad_gate, grad_up, grad_down)


def on_device_rows(queries, keys, values, lr_codes, fast_gate, fast_up, fast_down):
    token_rates = (lr_codes.astype(jnp.float32) + 1.0) / 16.0
    target = (-token_rates[:, :, None] * values.astype(jnp.float32)).astype(jnp.bfloat16)
    gate_b, up_b, down_b = (
        lax.all_gather(fast_gate.astype(jnp.bfloat16), ("seq", "sub"), axis=1, tiled=True),
        lax.all_gather(fast_up.astype(jnp.bfloat16), ("seq", "sub"), axis=1, tiled=True),
        lax.all_gather(fast_down.astype(jnp.bfloat16), ("seq", "sub"), axis=1, tiled=True),
    )
    grad_gate, grad_up, grad_down = local_grads_rows(keys, target, gate_b, up_b, down_b)
    owned = (
        lax.psum_scatter(grad_gate, ("seq", "sub"), scatter_dimension=1, tiled=True),
        lax.psum_scatter(grad_up, ("seq", "sub"), scatter_dimension=1, tiled=True),
        lax.psum_scatter(grad_down, ("seq", "sub"), scatter_dimension=1, tiled=True),
    )
    weights = (fast_gate, fast_up, fast_down)
    grad_local = jnp.stack(
        [
            jnp.sum(owned[0] * owned[0], axis=(1, 2)),
            jnp.sum(owned[1] * owned[1], axis=(1, 2)),
            jnp.sum(owned[2] * owned[2], axis=(1, 2)),
        ],
        axis=1,
    )
    col_gate, col_up, col_down, grad_totals = lax.psum(
        (column_squares(fast_gate), column_squares(fast_up), column_squares(fast_down), grad_local),
        ("seq", "sub"),
    )
    col_weights = (col_gate, col_up, col_down)
    moved_all = []
    for index in range(3):
        scale = step_scale(col_weights[index], grad_totals[:, index])
        moved_all.append(weights[index] - scale[:, None, None] * owned[index])
    moved_cols = lax.psum(
        (column_squares(moved_all[0]), column_squares(moved_all[1]), column_squares(moved_all[2])),
        ("seq", "sub"),
    )
    renewed = [
        rescale(moved_all[index], col_weights[index], moved_cols[index]).astype(jnp.bfloat16)
        for index in range(3)
    ]
    new_gate, new_up, new_down = (
        lax.all_gather(renewed[0], ("seq", "sub"), axis=1, tiled=True),
        lax.all_gather(renewed[1], ("seq", "sub"), axis=1, tiled=True),
        lax.all_gather(renewed[2], ("seq", "sub"), axis=1, tiled=True),
    )
    return apply_rows(queries, new_gate, new_up, new_down)


def solution(mesh):
    groups, seq, sub = (mesh.shape[axis] for axis in ("groups", "seq", "sub"))

    def on_device(*arrays):
        if groups == 2 and sub == 2 and seq % (2 * WIDTH) == 0 and arrays[4].shape[0] == seq:
            return on_device_heads(seq // WIDTH, *arrays)
        return on_device_rows(*arrays)

    return jax.shard_map(
        on_device,
        mesh=mesh,
        in_specs=(
            P("head", ("groups", "seq", "sub"), None),
            P("head", ("groups", "seq", "sub"), None),
            P("head", ("groups", "seq", "sub"), None),
            P("head", ("groups", "seq", "sub")),
            P("head", ("seq", "sub"), None),
            P("head", ("seq", "sub"), None),
            P("head", ("seq", "sub"), None),
        ),
        out_specs=P("head", ("groups", "seq", "sub"), None),
        check_vma=False,
    )
```

profile of v0, /device:TPU:0, one launch (start us, length us, event | category | flops | bytes accessed | tf_op | source)
XLA Modules:
  0.0 256.1 jit_solution(11082226915661433239)
XLA Ops:
  0.0 1.4 broadcast_in_dim.3.codes
  1.4 1.1 convert_bitcast_fusion.2
  2.5 1.3 convert_bitcast_fusion
  3.7 0.9 fusion.13.own
  4.7 155.6 %learn.1 = (f32[3,512,256]{2,1,0:T(8,128)}, bf16[3,512,512]{2,1,0:T(8,128)(2,1)}) custom-call(bf16[8,3,32,512]{3,2,1,0:T(8,128)(2,1)} %fusion.13.own, bf16[8,1024,512]{2,1,0:T(8,128)(2,1)} %keys.1, bf16[8,1024,512]{2,1,0:T(8,128)(2,1)} %values.1, s32[8,1,1024]{2,1,0:T(1,128)} %broadcast_in_dim.3.codes), custom_call_target="tpu_custom_call" | custom-call | tf_op jit(solution)/shard_map/learn/pallas_call | solution.py:308
  160.3 77.6 %renew.1 = bf16[4,2,2,3,512,256]{5,4,3,2,1,0:T(8,128)(2,1)} custom-call(f32[3,512,256]{2,1,0:T(8,128)} %get-tuple-element.7.total, bf16[3,512,512]{2,1,0:T(8,128)(2,1)} %get-tuple-element.8.weights), custom_call_target="tpu_custom_call" | custom-call | tf_op jit(solution)/shard_map/renew/pallas_call | solution.py:459
  237.9 18.2 %apply.1 = bf16[8,1024,512]{2,1,0:T(8,128)(2,1)} custom-call(bf16[8,1024,512]{2,1,0:T(8,128)(2,1)} %queries.1, bf16[8,2,3,512,256]{4,3,2,1,0:T(8,128)(2,1)} %bitcast.7), custom_call_target="tpu_custom_call" | custom-call | tf_op jit(solution)/shard_map/apply/pallas_call | solution.py:359
where the time goes:
time: 257 us; the launch traced here: 256 us
  Pallas kernels  251 us (98%)
  other arithmetic  3.28 us (1%)
    pallas_call x1, Pallas kernels, learn(): pl.pallas_call(functools.partial(gather_kernel, depth), out_shape=(jax.Sh...  156 us
    pallas_call x1, Pallas kernels, renew(): pl.pallas_call(functools.partial(renew_kernel, depth), out_shape=jax.Shap...  77.6 us
    pallas_call x1, Pallas kernels, apply_fast(): pl.pallas_call(apply_kernel, grid=(heads,), out_shape=jax.ShapeDtypeStruc...  18.2 us

commit v1 on v0

v1 whole, which is shorter than its diff:
```python
import functools

import jax
import jax.numpy as jnp
from jax import lax
from jax.experimental import pallas as pl
from jax.experimental.pallas import tpu as pltpu
from jax.sharding import PartitionSpec as P

EPSILON = 1e-06
STEP_SIZE = 0.5
WIDTH = 2
DEPTH = 4
VMEM_LIMIT = 54 * 1024 * 1024
BF = jnp.bfloat16
F32 = jnp.float32


def place_of(z):
    return jnp.where(2 * z < DEPTH, 2 * z, 2 * (DEPTH - 1 - z) + 1)


def device(z, x, s):
    return {"seq": z * WIDTH + x, "sub": s}


def greet(partners):
    barrier = pltpu.get_barrier_semaphore()
    for partner in partners:
        pl.semaphore_signal(barrier, inc=1, device_id=partner, device_id_type=pl.DeviceIdType.MESH)
    pl.semaphore_wait(barrier, len(partners))


def send(src, dst, send_sem, recv_sem, target):
    return pltpu.make_async_remote_copy(
        src_ref=src,
        dst_ref=dst,
        send_sem=send_sem,
        recv_sem=recv_sem,
        device_id=target,
        device_id_type=pl.DeviceIdType.MESH,
    )


def dot(a, b, dims=((1,), (0,))):
    return lax.dot_general(a, b, (dims, ((), ())), preferred_element_type=F32)


def owner(k):
    return jnp.where(k % 2 == 0, k // 2, DEPTH - 1 - k // 2)


def gather_units(rows):
    part = rows // 2
    return ((0, 0, rows, False), (1, 0, rows, False), (2, 0, part, False), (2, part, rows - part, True))


def step_kernel(
    gate_w, up_w, down_w, codes, keys, values, queries, out,
    full, stage, rates, tok, gsend, got_x, kept, zsum, got_z, new, norm_out, norm_in,
    ps, pr, cs, cr, ll, ls, lr, free,
    gs, gr, xs, xr, ys, yr,
    rxs, rxr, rzs, rzr, ns, nr,
    hsl, hsr, hr, fs, fr, os, orr,
):
    n = DEPTH
    z, x = lax.div(lax.axis_index("seq"), WIDTH), lax.rem(lax.axis_index("seq"), WIDTH)
    s, y = lax.axis_index("sub"), lax.axis_index("groups")
    feats = gate_w.shape[2]
    half = feats // 2
    mate, side = device(z, x, 1 - s), device(z, 1 - x, s)
    units = gather_units(feats)

    def cols(j):
        return pl.ds(pl.multiple_of(j * half, half), half)

    def here(src, g, i, k):
        return pltpu.make_async_copy(src.at[2 * k + s], tok.at[2 * lax.rem(g, 2) + i, s], ll.at[g, i])

    def there(src, g, i, k):
        return send(
            src.at[2 * k + 1 - s], tok.at[2 * lax.rem(g, 2) + i, s], ls.at[g, i], lr.at[g, i], mate
        )

    def load(g, what):
        def learning():
            what(keys, g, 0, g).start()
            what(values, g, 1, g).start()

        def applying():
            for i in range(2):
                what(queries, g, i, 2 * (g - n) + i).start()

        if isinstance(g, int):
            learning() if g < n else applying()
        else:
            pl.when(g < n)(learning)
            pl.when(g >= n)(applying)

    def loaded(g, i):
        here(keys, g, i, 0).wait()
        there(keys, g, i, 0).wait_recv()

    def pair(k):
        return send(stage.at[k], full.at[k, :, z, x, s], ps.at[k], pr.at[k], mate)

    def paired(k):
        block = full.at[k, :, z, x, 1 - s]
        return send(stage.at[k], block, ps.at[k], pr.at[k], mate)

    def along(k, zt):
        block = full.at[k, :, z, x, y]
        return send(block, block, gs.at[k, zt], gr.at[k, z], device(zt, x, s))

    def along_in(k, src):
        block = full.at[k, :, src, x, y]
        return send(block, block, gs.at[k, src], gr.at[k, src], device(src, x, s))

    def across(k, src, col):
        block = full.at[k, :, src, col, y]
        return send(block, block, xs.at[k, src], xr.at[k, src], side)

    def over(k, src, col, row):
        block = full.at[k, :, src, col, row]
        return send(block, block, ys.at[k, src, col], yr.at[k, src, col], {"groups": 1 - y})

    def others():
        return [lax.rem(z + d, n) for d in range(1, n)]

    def first(k):
        paired(k).wait_recv()
        for zt in others():
            along(k, zt).start()
        across(k, z, x).start()

    def second(k):
        for src in others():
            along_in(k, src).wait_recv()
            across(k, src, x).start()
            over(k, src, x, y).start()

    def third(k):
        for src in [z] + others():
            across(k, src, 1 - x).wait_recv()
            over(k, src, 1 - x, y).start()

    def swap(k, m):
        return send(gsend.at[k, m], got_x.at[k, m], rxs.at[k, m], rxr.at[k, m], side)

    def compute(k):
        for src in [z] + others():
            over(k, src, 1 - x, 1 - y).wait_recv()
        for src in others():
            over(k, src, x, 1 - y).wait_recv()
        for i in range(2):
            loaded(k, i)
        slot = 2 * lax.rem(k, 2)
        tokens = tok.shape[2]
        for c in range(2):
            rate = (rates[c, pl.ds(2 * k + s, 1), :].astype(F32) + 1.0) / 16.0
            rate = jnp.transpose(jnp.broadcast_to(rate, (128, tokens)))
            rate = jnp.concatenate([rate] * (feats // 128), axis=1)
            tok[slot + 1, c] = (-rate * tok[slot + 1, c].astype(F32)).astype(BF)
        for step, j in enumerate((1 - x, x)):
            gate = full[k, 0, :, :, :, :, cols(j)].reshape(feats, half)
            up = full[k, 1, :, :, :, :, cols(j)].reshape(feats, half)
            down = full[k, 2, pl.ds(j * (n // 2), n // 2)].reshape(half, feats)
            sums = [None] * 4
            for c in range(2):
                key, target = tok[slot, c], tok[slot + 1, c]
                gate_pre = dot(key, gate)
                up_pre = dot(key, up)
                back = dot(target, down, ((1,), (1,)))
                sig = jax.nn.sigmoid(gate_pre)
                silu = gate_pre * sig
                hidden = (silu * up_pre).astype(BF)
                ggp = (back * up_pre * sig * (1.0 + gate_pre * (1.0 - sig))).astype(BF)
                gup = (back * silu).astype(BF)
                terms = (
                    dot(key, ggp, ((0,), (0,))),
                    dot(key, gup, ((0,), (0,))),
                    dot(hidden, tok[slot + 1, c, :, cols(1 - x)], ((0,), (0,))),
                    dot(hidden, tok[slot + 1, c, :, cols(x)], ((0,), (0,))),
                )
                sums = [t if a is None else a + t for a, t in zip(sums, terms)]
            gsend[k, 2, cols(j), :] = sums[2].astype(BF)
            kept[k, 2, cols(j), :] = sums[3]
            for m in range(2):
                if step == 0:
                    gsend[k, m] = sums[m].astype(BF)
                    swap(k, m).start()
                else:
                    kept[k, m] = sums[m]
        swap(k, 2).start()
        pl.semaphore_signal(free, inc=1, device_id=mate, device_id_type=pl.DeviceIdType.MESH)
        load(k + 2, here)

    def refill(k):
        pl.semaphore_wait(free, 1)
        load(k + 2, there)

    def toward(k, m):
        return send(
            zsum.at[k, m], got_z.at[z, m], rzs.at[k, m], rzr.at[z, m], device(owner(k), x, s)
        )

    def summed(src, m):
        block = got_z.at[src, m]
        return send(block, block, rzs.at[0, m], rzr.at[src, m], device(src, x, s))

    def combine(k):
        for m in range(3):
            swap(k, m).wait_recv()

            @pl.when(z == owner(k))
            def _(m=m):
                kept[k, m] += got_x[k, m].astype(F32)

            @pl.when(z != owner(k))
            def _(m=m):
                zsum[k, m] = (kept[k, m] + got_x[k, m].astype(F32)).astype(BF)
                toward(k, m).start()

    def block(k, u, col):
        m, begin, count, _ = units[u]
        return new.at[k, col, m, pl.ds(begin, count)]

    def hop(k, u, c, onward):
        piece = block(k, u, 1 - x if c else x)
        sems = hsr if onward == 1 else hsl
        return send(piece, piece, sems.at[k, u, c], hr.at[k, u, c], device(z + onward, x, s))

    def share(k, u, out_col):
        piece = block(k, u, out_col)
        return send(piece, piece, fs.at[k, u], fr.at[k, u], side)

    def spread(k, u, c):
        pl.when(z > 0)(lambda: hop(k, u, c, -1).start())
        pl.when(z < n - 1)(lambda: hop(k, u, c, 1).start())

    def renew(k):
        def norms(m):
            return send(norm_out.at[m], norm_in.at[m], ns.at[m], nr.at[m], side)

        def own(m):
            return full[k, m, :, :, :, :, cols(x)].reshape(feats, half).astype(F32)

        weight_totals, col_weights = [], []
        for m in range(3):
            whole = full[k, m].reshape(feats, feats).astype(F32)
            weight_totals.append(jnp.sum(whole * whole, keepdims=True))
            col_weights.append(jnp.sum(own(m) * own(m), axis=0, keepdims=True))

        def gather(m):
            for src in others():
                summed(src, m).wait_recv()
                kept[k, m] += got_z[src, m].astype(F32)
            part = kept[k, m]
            norm_out[m] = jnp.broadcast_to(jnp.sum(part * part, keepdims=True), norm_out.shape[1:])
            norms(m).start()

        def move(m):
            norms(m).wait()
            grad_total = norm_out[m, :1, :1] + norm_in[m, :1, :1]
            scale = STEP_SIZE * jnp.sqrt(weight_totals[m] + EPSILON) / jnp.sqrt(grad_total + EPSILON)
            moved = own(m) - scale * kept[k, m]
            col_moved = jnp.sum(moved * moved, axis=0, keepdims=True)
            ratio = jnp.sqrt((col_weights[m] + EPSILON) / (col_moved + EPSILON))
            new[k, x, m] = (moved * ratio).astype(BF)
            for u in reversed(range(len(units))):
                if units[u][0] == m:
                    share(k, u, x).start()
                    if not units[u][3]:
                        spread(k, u, 0)

        gather(0)
        gather(1)
        move(0)
        gather(2)
        move(1)
        move(2)
        spread(k, 3, 0)
        share(k, 3, 1 - x).wait_recv()
        spread(k, 3, 1)

    def relay(d, u, c, early):
        for onward in (1, -1):
            src = z - d * onward
            end = (d == 1) & ((src == 0) | (src == n - 1))
            there = (src >= 0) & (src < n)

            @pl.when(there & (end if early else jnp.logical_not(end)))
            def _(src=src, onward=onward):
                k = place_of(src)
                hop(k, u, c, 0).wait_recv()

                @pl.when((z + onward >= 0) & (z + onward < n))
                def _():
                    hop(k, u, c, onward).start()

                if not units[u][3]:
                    share(k, u, x).start()

    def result(k, h):
        return send(tok.at[k, 1 - s], out.at[h], os.at[k], orr.at[k], mate)

    def apply(k):
        for u in range(3):
            share(k, u, 1 - x).wait_recv()
        for i in range(2):
            pl.when(lax.rem(k, 2) == i)(lambda i=i: loaded(n + k // 2, i))
        for step, c in enumerate((1 - s, s)):
            q = tok[k, c]
            total = [None, None]
            for j in range(2):
                gate = dot(q, new[k, j, 0])
                up = dot(q, new[k, j, 1])
                hidden = (gate * jax.nn.sigmoid(gate) * up).astype(BF)
                for i in range(2):
                    term = dot(hidden, new[k, i, 2, pl.ds(j * half, half), :])
                    total[i] = term if j == 0 else total[i] + term
            for i in range(2):
                if step == 0:
                    tok[k, 1 - s, :, pl.ds(i * half, half)] = total[i].astype(BF)
                else:
                    out[2 * k + s, :, pl.ds(i * half, half)] = total[i].astype(BF)
            if step == 0:
                result(k, 2 * k + s).start()

    for g in range(2):
        load(g, here)
    for k in range(n):
        for m, weight in enumerate((gate_w, up_w, down_w)):
            full[k, m, z, x, s] = weight[2 * k + s].astype(BF)
            stage[k, m] = weight[2 * k + 1 - s].astype(BF)
    rates[s] = codes[...]
    greet([device(zt, x, s) for zt in others()] + [side, mate, {"groups": 1 - y}])
    for k in range(n):
        pair(k).start()
    coded = send(codes, rates.at[s], cs, cr, mate)
    coded.start()
    for g in range(2):
        load(g, there)
    send(codes, rates.at[1 - s], cs, cr, mate).wait_recv()
    for k in range(n):
        first(k)

    def bring(k, carry):
        second(k)
        pl.when(k < n - 1)(lambda: third(k))
        return carry

    lax.fori_loop(0, n, bring, 0)

    def step(t, carry):
        def when(k, what):
            pl.when((k >= 0) & (k < n))(lambda: what(k))

        when(t, compute)
        pl.when(t == 0)(lambda: third(n - 1))
        when(t, refill)
        when(t - 1, combine)
        return carry

    lax.fori_loop(0, n + 1, step, 0)

    for u in range(len(units)):
        for c in range(2 if units[u][3] else 1):
            relay(1, u, c, True)
    renew(place_of(z))

    def outward(d, carry):
        @pl.when(d < n - 1)
        def _():
            for u in range(len(units)):
                for c in range(2 if units[u][3] else 1):
                    relay(d + 1, u, c, False)

        def at(i, carry):
            src = z + d * (1 - 2 * i)

            @pl.when((src >= 0) & (src < n) & ((d > 0) | (i == 0)))
            def _():
                apply(place_of(src))

            return carry

        return lax.fori_loop(0, 2, at, carry)

    lax.fori_loop(0, n, outward, 0)

    def last(k, carry):
        pair(k).wait_send()
        for zt in others():
            along(k, zt).wait_send()
        for src in [z] + others():
            across(k, src, x).wait_send()
            over(k, src, 1 - x, y).wait_send()
        for src in others():
            over(k, src, x, y).wait_send()
        for m in range(3):
            swap(k, m).wait_send()
            pl.when(z != owner(k))(lambda m=m: toward(k, m).wait_send())
        for u in range(len(units)):
            for c in range(2 if units[u][3] else 1):
                pl.when((z >= owner(k)) & (z < n - 1))(lambda u=u, c=c: hop(k, u, c, 1).wait_send())
                pl.when((z <= owner(k)) & (z > 0))(lambda u=u, c=c: hop(k, u, c, -1).wait_send())
            if not units[u][3]:
                share(k, u, x).wait_send()
            else:
                pl.when(z == owner(k))(lambda u=u: share(k, u, x).wait_send())
        result(k, 2 * k + 1 - s).wait()
        return carry

    lax.fori_loop(0, n, last, 0)
    for g in range(n + n // 2):
        for i in range(2):
            there(keys, g, i, 0).wait_send()
    coded.wait_send()


def whole_step(queries, keys, values, codes, gate_w, up_w, down_w):
    heads, rows, feats = gate_w.shape
    tokens = keys.shape[1]
    n = DEPTH
    half = feats // 2
    dma = pltpu.SemaphoreType.DMA
    vmem = pl.BlockSpec(memory_space=pltpu.VMEM)
    anywhere = pl.BlockSpec(memory_space=pl.ANY)
    piece = (3, feats, half)
    count = len(gather_units(feats))
    return pl.pallas_call(
        step_kernel,
        out_shape=pltpu.VMEM((heads, tokens, feats), BF),
        in_specs=[vmem] * 4 + [anywhere] * 3,
        out_specs=vmem,
        scratch_shapes=[
            pltpu.VMEM((n, 3, n, WIDTH, 2, rows, feats), BF),
            pltpu.VMEM((n, 3, rows, feats), BF),
            pltpu.VMEM((2, heads, tokens), jnp.int32),
            pltpu.VMEM((4, 2, tokens, feats), BF),
            pltpu.VMEM((n,) + piece, BF),
            pltpu.VMEM((n,) + piece, BF),
            pltpu.VMEM((n,) + piece, F32),
            pltpu.VMEM((n,) + piece, BF),
            pltpu.VMEM((n,) + piece, BF),
            pltpu.VMEM((n, 2) + piece, BF),
            pltpu.VMEM((3, 8, 128), F32),
            pltpu.VMEM((3, 8, 128), F32),
            dma((n,)), dma((n,)), dma(()), dma(()),
            *[dma((n + n // 2, 2))] * 3,
            pltpu.SemaphoreType.REGULAR,
            *[dma((n, n))] * 4,
            *[dma((n, n, WIDTH))] * 2,
            *[dma((n, 3))] * 4,
            *[dma((3,))] * 2,
            *[dma((n, count, 2))] * 3,
            *[dma((n, count))] * 2,
            *[dma((n,))] * 2,
        ],
        compiler_params=pltpu.CompilerParams(
            collective_id=0, has_side_effects=True, vmem_limit_bytes=VMEM_LIMIT
        ),
        name="whole_step",
    )(gate_w, up_w, down_w, codes, keys, values, queries)


def column_squares(matrix):
    return jnp.sum(matrix * matrix, axis=1)


def rescale(moved, col_weight, col_moved):
    return moved * jnp.sqrt((col_weight + EPSILON) / (col_moved + EPSILON))[:, None, :]


def step_scale(col_weight, grad_total):
    return (
        STEP_SIZE * jnp.sqrt(jnp.sum(col_weight, axis=1) + EPSILON) / jnp.sqrt(grad_total + EPSILON)
    )


def apply_rows(queries, gate_b, up_b, down_b):
    query_gate = jnp.einsum("htd,hdf->htf", queries, gate_b, preferred_element_type=jnp.float32)
    query_up = jnp.einsum("htd,hdf->htf", queries, up_b, preferred_element_type=jnp.float32)
    query_hidden = (jax.nn.silu(query_gate) * query_up).astype(jnp.bfloat16)
    return jnp.einsum(
        "htf,hfd->htd", query_hidden, down_b, preferred_element_type=jnp.float32
    ).astype(jnp.bfloat16)


def local_grads_rows(keys, target, gate_b, up_b, down_b):
    gate_pre = jnp.einsum("htd,hdf->htf", keys, gate_b, preferred_element_type=jnp.float32)
    up_pre = jnp.einsum("htd,hdf->htf", keys, up_b, preferred_element_type=jnp.float32)
    sigmoid_gate = jax.nn.sigmoid(gate_pre)
    hidden = (gate_pre * sigmoid_gate * up_pre).astype(jnp.bfloat16)
    back = jnp.einsum("htd,hfd->htf", target, down_b, preferred_element_type=jnp.float32)
    grad_gate_pre = (back * up_pre * sigmoid_gate * (1.0 + gate_pre * (1.0 - sigmoid_gate))).astype(
        jnp.bfloat16
    )
    grad_up_pre = (back * gate_pre * sigmoid_gate).astype(jnp.bfloat16)
    grad_gate = jnp.einsum("htd,htf->hdf", keys, grad_gate_pre, preferred_element_type=jnp.float32)
    grad_up = jnp.einsum("htd,htf->hdf", keys, grad_up_pre, preferred_element_type=jnp.float32)
    grad_down = jnp.einsum("htf,htd->hfd", hidden, target, preferred_element_type=jnp.float32)
    return (grad_gate, grad_up, grad_down)


def on_device_rows(queries, keys, values, lr_codes, fast_gate, fast_up, fast_down):
    token_rates = (lr_codes.astype(jnp.float32) + 1.0) / 16.0
    target = (-token_rates[:, :, None] * values.astype(jnp.float32)).astype(jnp.bfloat16)
    gate_b, up_b, down_b = (
        lax.all_gather(fast_gate.astype(jnp.bfloat16), ("seq", "sub"), axis=1, tiled=True),
        lax.all_gather(fast_up.astype(jnp.bfloat16), ("seq", "sub"), axis=1, tiled=True),
        lax.all_gather(fast_down.astype(jnp.bfloat16), ("seq", "sub"), axis=1, tiled=True),
    )
    grad_gate, grad_up, grad_down = local_grads_rows(keys, target, gate_b, up_b, down_b)
    owned = (
        lax.psum_scatter(grad_gate, ("seq", "sub"), scatter_dimension=1, tiled=True),
        lax.psum_scatter(grad_up, ("seq", "sub"), scatter_dimension=1, tiled=True),
        lax.psum_scatter(grad_down, ("seq", "sub"), scatter_dimension=1, tiled=True),
    )
    weights = (fast_gate, fast_up, fast_down)
    grad_local = jnp.stack(
        [
            jnp.sum(owned[0] * owned[0], axis=(1, 2)),
            jnp.sum(owned[1] * owned[1], axis=(1, 2)),
            jnp.sum(owned[2] * owned[2], axis=(1, 2)),
        ],
        axis=1,
    )
    col_gate, col_up, col_down, grad_totals = lax.psum(
        (column_squares(fast_gate), column_squares(fast_up), column_squares(fast_down), grad_local),
        ("seq", "sub"),
    )
    col_weights = (col_gate, col_up, col_down)
    moved_all = []
    for index in range(3):
        scale = step_scale(col_weights[index], grad_totals[:, index])
        moved_all.append(weights[index] - scale[:, None, None] * owned[index])
    moved_cols = lax.psum(
        (column_squares(moved_all[0]), column_squares(moved_all[1]), column_squares(moved_all[2])),
        ("seq", "sub"),
    )
    renewed = [
        rescale(moved_all[index], col_weights[index], moved_cols[index]).astype(jnp.bfloat16)
        for index in range(3)
    ]
    new_gate, new_up, new_down = (
        lax.all_gather(renewed[0], ("seq", "sub"), axis=1, tiled=True),
        lax.all_gather(renewed[1], ("seq", "sub"), axis=1, tiled=True),
        lax.all_gather(renewed[2], ("seq", "sub"), axis=1, tiled=True),
    )
    return apply_rows(queries, new_gate, new_up, new_down)


def solution(mesh):
    groups, seq, sub = (mesh.shape[axis] for axis in ("groups", "seq", "sub"))

    def on_device(*arrays):
        if groups == 2 and sub == 2 and seq == WIDTH * DEPTH and arrays[4].shape[0] == 2 * DEPTH:
            return whole_step(*arrays)
        return on_device_rows(*arrays)

    return jax.shard_map(
        on_device,
        mesh=mesh,
        in_specs=(
            P("head", ("groups", "seq", "sub"), None),
            P("head", ("groups", "seq", "sub"), None),
            P("head", ("groups", "seq", "sub"), None),
            P("head", ("groups", "seq", "sub")),
            P("head", ("seq", "sub"), None),
            P("head", ("seq", "sub"), None),
            P("head", ("seq", "sub"), None),
        ),
        out_specs=P("head", ("groups", "seq", "sub"), None),
        check_vma=False,
    )
```

time: 257 us -> 229 us (0.89)
  Pallas kernels: 251 us -> 226 us
  other arithmetic: 3.28 us -> 0 us
    pallas_call x3 -> x1, Pallas kernels: 251 us -> 226 us  [whole_step(): pl.pallas_call(step_kernel, out_shape=pltpu.VMEM((heads, tokens, feats),...]
    unnamed x0 -> x1, local copies, waits for them, and re-layouts: none -> 3.4 us
    another operation x3 -> x0, other arithmetic: 3.28 us -> none  [the longest x2 2.34 us: on_device_heads(): own = jnp.stack([fast_gate, fast_down, fast_up], axis=1).astype(BF)]
where the time goes in v1:
time: 229 us
  Pallas kernels  226 us (99%)
  local copies, waits for them, and re-layouts  3.4 us (1%)
    pallas_call x1, Pallas kernels, whole_step(): pl.pallas_call(step_kernel, out_shape=pltpu.VMEM((heads, tokens, feats),...  226 us

profile of v1, /device:TPU:0, one launch (start us, length us, event | category | flops | bytes accessed | tf_op | source)
XLA Modules:
  0.0 229.0 jit_solution(10322230423215974761)
XLA Ops:
  0.0 225.6 %whole_step.1 = bf16[8,1024,512]{2,1,0:T(8,128)(2,1)S(1)} custom-call(f32[8,32,512]{2,1,0:T(8,128)} %gate_w.1, f32[8,32,512]{2,1,0:T(8,128)} %up_w.1, f32[8,32,512]{2,1,0:T(8,128)} %down_w.1, s32[8,1024]{1,0:T(8,128)} %codes.1, bf16[8,1024,512]{2,1,0:T(8,128)(2,1)} %keys.1, bf16[8,1024,512]{2,1,0:T(8,128)(2,1)} %values.1, bf16[8,1024,512]{2,1,0:T(8,128)(2,1)} %queries.1), custom_call_target="tpu_custom_call" | custom-call | tf_op jit(solution)/shard_map/whole_step/pallas_call | solution.py:432
  225.6 3.4 %copy.9 = bf16[8,1024,512]{2,1,0:T(8,128)(2,1)} copy(bf16[8,1024,512]{2,1,0:T(8,128)(2,1)S(1)} %whole_step.1) | data formatting | bytes 16777216

commit v2 on v1

--- a/solution.py
+++ b/solution.py
@@ -57,10 +57,10 @@
 
 def step_kernel(
     gate_w, up_w, down_w, codes, keys, values, queries, out,
-    full, stage, rates, tok, gsend, got_x, kept, zsum, got_z, new, norm_out, norm_in,
+    full, stage, rates, tok, gsend, got_x, kept, zsum, got_m, got_z, new, norm_out, norm_in,
     ps, pr, cs, cr, ll, ls, lr, free,
     gs, gr, xs, xr, ys, yr,
-    rxs, rxr, rzs, rzr, ns, nr,
+    rxs, rxr, rzs, rmr, rzr, ns, nr,
     hsl, hsr, hr, fs, fr, os, orr,
 ):
     n = DEPTH
@@ -191,7 +191,7 @@
                     swap(k, m).start()
                 else:
                     kept[k, m] = sums[m]
-        swap(k, 2).start()
+        descend(k)
         pl.semaphore_signal(free, inc=1, device_id=mate, device_id_type=pl.DeviceIdType.MESH)
         load(k + 2, here)
 
@@ -199,27 +199,59 @@
         pl.semaphore_wait(free, 1)
         load(k + 2, there)
 
-    def toward(k, m):
+    def far(k):
+        return jnp.where(2 * owner(k) < n, n - 1, 0)
+
+    def middle(k):
+        return jnp.where(2 * owner(k) < n, n - 2, 1)
+
+    def leaving(k, m):
+        return zsum.at[k, m] if m < 3 else gsend.at[k, 2]
+
+    def inward(k, m):
         return send(
-            zsum.at[k, m], got_z.at[z, m], rzs.at[k, m], rzr.at[z, m], device(owner(k), x, s)
+            leaving(k, m), got_m.at[k // 2, m], rzs.at[k, m], rmr.at[k // 2, m], device(middle(k), x, s)
         )
 
-    def summed(src, m):
-        block = got_z.at[src, m]
-        return send(block, block, rzs.at[0, m], rzr.at[src, m], device(src, x, s))
+    def toward(k, m, slot):
+        return send(
+            leaving(k, m), got_z.at[slot, m], rzs.at[k, m], rzr.at[slot, m], device(owner(k), x, s)
+        )
+
+    def leave(k, m):
+        pl.when(z == far(k))(lambda: inward(k, m).start())
+        pl.when(z != far(k))(lambda: toward(k, m, 1).start())
+
+    def descend(k):
+        @pl.when((z != owner(k)) & (z != middle(k)))
+        def _():
+            zsum[k, 2] = kept[k, 2].astype(BF)
+            leave(k, 2)
+            leave(k, 3)
 
     def combine(k):
-        for m in range(3):
+        for m in range(2):
             swap(k, m).wait_recv()
 
-            @pl.when(z == owner(k))
+            @pl.when((z == owner(k)) | (z == middle(k)))
             def _(m=m):
                 kept[k, m] += got_x[k, m].astype(F32)
 
-            @pl.when(z != owner(k))
+            @pl.when((z != owner(k)) & (z != middle(k)))
             def _(m=m):
                 zsum[k, m] = (kept[k, m] + got_x[k, m].astype(F32)).astype(BF)
-                toward(k, m).start()
+                leave(k, m)
+
+    def bridge(k):
+        @pl.when(z == middle(k))
+        def _():
+            for m in (2, 3, 0, 1):
+                inward(k, m).wait_recv()
+                if m < 3:
+                    zsum[k, m] = (kept[k, m] + got_m[k // 2, m].astype(F32)).astype(BF)
+                else:
+                    gsend[k, 2] = (gsend[k, 2].astype(F32) + got_m[k // 2, m].astype(F32)).astype(BF)
+                toward(k, m, 0).start()
 
     def block(k, u, col):
         m, begin, count, _ = units[u]
@@ -252,9 +284,11 @@
             col_weights.append(jnp.sum(own(m) * own(m), axis=0, keepdims=True))
 
         def gather(m):
-            for src in others():
-                summed(src, m).wait_recv()
-                kept[k, m] += got_z[src, m].astype(F32)
+            for slot in range(2):
+                toward(k, m, slot).wait_recv()
+                kept[k, m] += got_z[slot, m].astype(F32)
+
+        def measure(m):
             part = kept[k, m]
             norm_out[m] = jnp.broadcast_to(jnp.sum(part * part, keepdims=True), norm_out.shape[1:])
             norms(m).start()
@@ -267,29 +301,39 @@
             col_moved = jnp.sum(moved * moved, axis=0, keepdims=True)
             ratio = jnp.sqrt((col_weights[m] + EPSILON) / (col_moved + EPSILON))
             new[k, x, m] = (moved * ratio).astype(BF)
+            for u in range(len(units)):
+                if units[u][0] == m:
+                    if not units[u][3]:
+                        spread(k, u, 0)
             for u in reversed(range(len(units))):
                 if units[u][0] == m:
                     share(k, u, x).start()
-                    if not units[u][3]:
-                        spread(k, u, 0)
-
+
+        for slot in range(2):
+            toward(k, 3, slot).wait_recv()
+        both = got_z[0, 3].astype(F32) + got_z[1, 3].astype(F32)
+        gsend[k, 2] = (gsend[k, 2].astype(F32) + both).astype(BF)
+        swap(k, 2).start()
         gather(0)
+        measure(0)
+        gather(2)
+        move(0)
         gather(1)
-        move(0)
-        gather(2)
+        measure(1)
+        swap(k, 2).wait_recv()
+        kept[k, 2] += got_x[k, 2].astype(F32)
+        measure(2)
         move(1)
         move(2)
         spread(k, 3, 0)
         share(k, 3, 1 - x).wait_recv()
         spread(k, 3, 1)
 
-    def relay(d, u, c, early):
+    def relay(d, u, c):
         for onward in (1, -1):
             src = z - d * onward
-            end = (d == 1) & ((src == 0) | (src == n - 1))
-            there = (src >= 0) & (src < n)
-
-            @pl.when(there & (end if early else jnp.logical_not(end)))
+
+            @pl.when((src >= 0) & (src < n))
             def _(src=src, onward=onward):
                 k = place_of(src)
                 hop(k, u, c, 0).wait_recv()
@@ -305,7 +349,7 @@
         return send(tok.at[k, 1 - s], out.at[h], os.at[k], orr.at[k], mate)
 
     def apply(k):
-        for u in range(3):
+        for u in range(len(units) - 1):
             share(k, u, 1 - x).wait_recv()
         for i in range(2):
             pl.when(lax.rem(k, 2) == i)(lambda i=i: loaded(n + k // 2, i))
@@ -359,33 +403,33 @@
         when(t, compute)
         pl.when(t == 0)(lambda: third(n - 1))
         when(t, refill)
+        when(t - 2, bridge)
         when(t - 1, combine)
         return carry
 
-    lax.fori_loop(0, n + 1, step, 0)
-
-    for u in range(len(units)):
-        for c in range(2 if units[u][3] else 1):
-            relay(1, u, c, True)
+    lax.fori_loop(0, n + 2, step, 0)
+
+    pieces = ((0, 0), (1, 0), (2, 0), (3, 0), (3, 1))
     renew(place_of(z))
 
     def outward(d, carry):
         @pl.when(d < n - 1)
         def _():
-            for u in range(len(units)):
-                for c in range(2 if units[u][3] else 1):
-                    relay(d + 1, u, c, False)
+            for u, c in pieces[:-1]:
+                relay(d + 1, u, c)
+
+        pl.when(d < n - 2)(lambda: relay(d + 1, *pieces[-1]))
 
         def at(i, carry):
             src = z + d * (1 - 2 * i)
-
-            @pl.when((src >= 0) & (src < n) & ((d > 0) | (i == 0)))
-            def _():
-                apply(place_of(src))
-
+            there = (src >= 0) & (src < n) & ((d > 0) | (i == 0))
+            pl.when(there)(lambda: apply(place_of(src)))
             return carry
 
-        return lax.fori_loop(0, 2, at, carry)
+        lax.fori_loop(0, 2, at, carry)
+
+        pl.when(d == n - 2)(lambda: relay(d + 1, *pieces[-1]))
+        return carry
 
     lax.fori_loop(0, n, outward, 0)
 
@@ -398,9 +442,11 @@
             over(k, src, 1 - x, y).wait_send()
         for src in others():
             over(k, src, x, y).wait_send()
-        for m in range(3):
+        for m in range(2):
             swap(k, m).wait_send()
-            pl.when(z != owner(k))(lambda m=m: toward(k, m).wait_send())
+        pl.when(z == owner(k))(lambda: swap(k, 2).wait_send())
+        for m in range(4):
+            pl.when(z != owner(k))(lambda m=m: toward(k, m, 0).wait_send())
         for u in range(len(units)):
             for c in range(2 if units[u][3] else 1):
                 pl.when((z >= owner(k)) & (z < n - 1))(lambda u=u, c=c: hop(k, u, c, 1).wait_send())
@@ -443,7 +489,8 @@
             pltpu.VMEM((n,) + piece, BF),
             pltpu.VMEM((n,) + piece, F32),
             pltpu.VMEM((n,) + piece, BF),
-            pltpu.VMEM((n,) + piece, BF),
+            pltpu.VMEM((2, 4, feats, half), BF),
+            pltpu.VMEM((2, 4, feats, half), BF),
             pltpu.VMEM((n, 2) + piece, BF),
             pltpu.VMEM((3, 8, 128), F32),
             pltpu.VMEM((3, 8, 128), F32),
@@ -452,7 +499,9 @@
             pltpu.SemaphoreType.REGULAR,
             *[dma((n, n))] * 4,
             *[dma((n, n, WIDTH))] * 2,
-            *[dma((n, 3))] * 4,
+            *[dma((n, 3))] * 2,
+            dma((n, 4)),
+            *[dma((2, 4))] * 2,
             *[dma((3,))] * 2,
             *[dma((n, count, 2))] * 3,
             *[dma((n, count))] * 2,

time: 229 us -> 210 us (0.917)
  Pallas kernels: 226 us -> 207 us
    pallas_call x1, Pallas kernels: 226 us -> 207 us  [whole_step(): pl.pallas_call(step_kernel, out_shape=pltpu.VMEM((heads, tokens, feats),...]
where the time goes in v2:
time: 210 us
  Pallas kernels  207 us (99%)
  local copies, waits for them, and re-layouts  3.4 us (2%)
    pallas_call x1, Pallas kernels, whole_step(): pl.pallas_call(step_kernel, out_shape=pltpu.VMEM((heads, tokens, feats),...  207 us

profile of v2, /device:TPU:0, one launch (start us, length us, event | category | flops | bytes accessed | tf_op | source)
XLA Modules:
  0.0 210.2 jit_solution(5357968520227367142)
XLA Ops:
  0.0 206.8 %whole_step.1 = bf16[8,1024,512]{2,1,0:T(8,128)(2,1)S(1)} custom-call(f32[8,32,512]{2,1,0:T(8,128)} %gate_w.1, f32[8,32,512]{2,1,0:T(8,128)} %up_w.1, f32[8,32,512]{2,1,0:T(8,128)} %down_w.1, s32[8,1024]{1,0:T(8,128)} %codes.1, bf16[8,1024,512]{2,1,0:T(8,128)(2,1)} %keys.1, bf16[8,1024,512]{2,1,0:T(8,128)(2,1)} %values.1, bf16[8,1024,512]{2,1,0:T(8,128)(2,1)} %queries.1), custom_call_target="tpu_custom_call" | custom-call | tf_op jit(solution)/shard_map/whole_step/pallas_call | solution.py:478
  206.8 3.4 %copy.9 = bf16[8,1024,512]{2,1,0:T(8,128)(2,1)} copy(bf16[8,1024,512]{2,1,0:T(8,128)(2,1)S(1)} %whole_step.1) | data formatting | bytes 16777216
